TPU v7x, 512 devices: a whole 4x8x8 slice. The times are simulated.
512 devices in a mesh: dp: 32 (over y, x), tensor: 16 (over z, core).
Axes of the slice: x: 4, y: 8, z: 8, core: 2. Of those that a mesh axis runs over, the one named last changes fastest.
Arguments:
- hidden_in: bfloat16 [2048, 12288], P('dp'), may hold values from -6 to 6
- norm_gain: bfloat16 [12288], replicated, may hold values from 0.099609375 to 1.8984375
- norm_shift: bfloat16 [12288], replicated, may hold values from -3 to 3
- up_weight: bfloat16 [12288, 24576], P('dp', 'tensor'), may hold values from -0.0546875 to 0.0546875
- up_bias: bfloat16 [24576], P('tensor'), may hold values from -3 to 3
- down_weight: bfloat16 [24576, 12288], P('tensor', 'dp'), may hold values from -0.09375 to 0.09375
- down_bias: bfloat16 [12288], P('tensor'), may hold values from -3 to 3
- active: int32 [64, 16, 4], P(None, 'tensor'), may hold values from 0 to 11, as said below
- counts: int32 [64, 16], P(None, 'tensor'), may hold values from 1 to 4, as said below
Outputs:
- hidden_out: bfloat16 [2048, 12288], P('dp', 'tensor')
Inputs may be any that keep to these rules, and one draw needn't show every extreme that they name: The 4 entries of each list are distinct; only the first counts entries are active. `counts`: every row group has a list with all 4 slots valid.
All inputs are finite; a program needn't handle non-finite values.
Results may differ from a plain program's by a relative error of at most 0.022.
Values may be sent and summed in bfloat16 or wider, within the bound.
No kernel may reach another device: no remote copies, remote signals or barrier semaphores. Data moves between devices by JAX's collectives and lax.ppermute only.
A program may use at most 64 MiB of HBM per device.

v0:
```python
import math
import jax
import jax.numpy as jnp
from jax import lax
from jax.sharding import PartitionSpec as P

BLOCK = 128
GROUP = 32


def in_blocks(step_fn, arrays):
    total = arrays[0].shape[0]
    per = math.gcd(total, 8)
    stacked = tuple((item.reshape((total // per, per) + item.shape[1:]) for item in arrays))
    result = lax.map(step_fn, stacked)
    return result.reshape((total,) + result.shape[2:])


def select_up(rows, ids, up_table):
    ngroups, slots = ids.shape
    grouped = rows.reshape(ngroups, -1, rows.shape[1])

    def step(pair):
        block_rows, block_ids = pair
        chosen = jnp.take(up_table, block_ids, axis=1)
        return jnp.einsum("grd,dgcb->grcb", block_rows, chosen, preferred_element_type=jnp.float32)

    result = in_blocks(step, (grouped, ids))
    return result.reshape(rows.shape[0], slots * up_table.shape[2])


def select_down(act, ids, down_table):
    ngroups, slots = ids.shape
    grouped = act.reshape(ngroups, -1, slots, down_table.shape[1])

    def step(pair):
        block_act, block_ids = pair
        chosen = jnp.take(down_table, block_ids, axis=0)
        return jnp.einsum("grcb,gcbd->grd", block_act, chosen, preferred_element_type=jnp.float32)

    result = in_blocks(step, (grouped, ids))
    return result.reshape(act.shape[0], down_table.shape[2])


def activate(pre, ids, valid, bias_table):
    ngroups, slots = ids.shape
    own = bias_table.shape[0]
    onehot = (ids[:, :, None] == jnp.arange(own, dtype=jnp.int32)[None, None, :]).astype(
        jnp.float32
    )
    bias_sel = jnp.einsum("gco,ob->gcb", onehot, bias_table, precision=lax.Precision.HIGHEST)
    mask = (jnp.arange(slots, dtype=jnp.int32)[None, :] < valid[:, None]).astype(jnp.float32)
    shaped = pre.reshape(ngroups, -1, slots, bias_table.shape[1])
    result = jnp.maximum(shaped + bias_sel[:, None], 0.0) * mask[:, None, :, None]
    return result.astype(jnp.bfloat16).reshape(pre.shape)


def body(
    hidden_in, norm_gain, norm_shift, up_weight, up_bias, down_weight, down_bias, active, counts
):
    row_dev = hidden_in.shape[0]
    values = hidden_in.astype(jnp.float32)
    center = values - jnp.mean(values, axis=-1, keepdims=True)
    spread = jnp.mean(center * center, axis=-1, keepdims=True)
    normed = (
        center * lax.rsqrt(spread + 1e-05) * norm_gain.astype(jnp.float32)
        + norm_shift.astype(jnp.float32)
    ).astype(jnp.bfloat16)
    columns = lax.all_to_all(normed, "dp", split_axis=1, concat_axis=0, tiled=True)
    d_part = up_weight.shape[0]
    own = up_weight.shape[1] // BLOCK
    up_table = up_weight.reshape(d_part, own, BLOCK)
    down_table = down_weight.reshape(own, BLOCK, d_part)
    bias_table = up_bias.astype(jnp.float32).reshape(own, BLOCK)
    ids = active[:, 0, :]
    valid = counts[:, 0]
    pre_own = lax.psum_scatter(
        select_up(columns, ids, up_table).astype(jnp.bfloat16),
        "dp",
        scatter_dimension=0,
        tiled=True,
    ).astype(jnp.float32)
    per_dev = row_dev // GROUP
    first = lax.axis_index("dp") * per_dev
    own_ids = lax.dynamic_slice_in_dim(ids, first, per_dev, 0)
    own_valid = lax.dynamic_slice_in_dim(valid, first, per_dev, 0)
    act_own = activate(pre_own, own_ids, own_valid, bias_table)
    act = lax.all_gather(act_own, "dp", axis=0, tiled=True)
    branch = select_down(act, ids, down_table)
    branch = branch.astype(jnp.bfloat16)
    returned = lax.all_to_all(branch, "dp", split_axis=0, concat_axis=1, tiled=True)
    summed = lax.psum_scatter(
        returned.astype(jnp.float32).astype(jnp.bfloat16), "tensor", scatter_dimension=1, tiled=True
    ).astype(jnp.float32)
    width = summed.shape[1]
    resid = lax.dynamic_slice_in_dim(hidden_in, lax.axis_index("tensor") * width, width, 1).astype(
        jnp.float32
    )
    return (resid + summed + down_bias.astype(jnp.float32)).astype(jnp.bfloat16)


def solution(mesh):
    placed = (
        P("dp", None),
        P(),
        P(),
        P("dp", "tensor"),
        P("tensor"),
        P("tensor", "dp"),
        P("tensor"),
        P(None, "tensor", None),
        P(None, "tensor"),
    )
    return jax.shard_map(
        body, mesh=mesh, in_specs=placed, out_specs=P("dp", "tensor"), check_vma=False
    )
```

profile of v0, /device:TPU:6, one launch (start us, length us, event | category | flops | bytes accessed | tf_op | source)
XLA Modules:
  0.0 595.1 jit_solution(5143126974400507887)
XLA Ops:
  6.5 1.8 convert_reduce_fusion
  8.4 0.6 fusion.28
  9.1 0.6 fusion.31
  9.8 1.4 copy.71
  11.2 10.4 %all-to-all-start = ((bf16[64,32,384]{2,0,1:T(8,128)(2,1)}), bf16[64,32,384]{2,0,1:T(8,128)(2,1)}, u32[]{:S(2)}, u32[]{:S(2)}) async-start(bf16[64,32,384]{2,0,1:T(8,128)(2,1)} %bitcast.85), calls=%async_computation | async-start | bytes 3145728 | tf_op jit(solution)/shard_map/all_to_all | solution.py:69
  21.7 1.4 copy.48
  23.2 1.7 copy.50
  24.9 36.1 %all-to-all-done = bf16[64,32,384]{2,0,1:T(8,128)(2,1)} async-done(((bf16[64,32,384]{2,0,1:T(8,128)(2,1)}), bf16[64,32,384]{2,0,1:T(8,128)(2,1)}, u32[]{:S(2)}, u32[]{:S(2)}) %all-to-all-start) | async-done | bytes 1572896 | tf_op jit(solution)/shard_map/all_to_all | solution.py:69
  60.9 51.3 %while.20 = (s32[]{:T(128)}, bf16[8,8,32,4,128]{4,2,3,1,0:T(8,128)(2,1)}, bf16[8,8,32,384]{3,2,1,0:T(8,128)(2,1)}, s32[8,8,4]{1,2,0:T(4,128)S(1)}, bf16[384,12,128]{2,0,1:T(8,128)(2,1)S(1)}, /*index=5*/s32[]{:T(128)}) while((s32[]{:T(128)}, bf16[8,8,32,4,128]{4,2,3,1,0:T(8,128)(2,1)}, bf16[8,8,32,384]{3,2,1,0:T(8,128)(2,1)}, ...), condition=%wide.region_3.4_spmd, body=%wide.region_2.3_spmd.sunk | while | flops 102237472 | bytes 10164557 | solution.py:15
  61.1 2.6 gather_fusion
  63.8 3.5 fusion.45
  67.5 2.6 gather_fusion
  70.1 0.1 copy.78
  70.2 3.5 fusion.45
  73.9 2.6 gather_fusion
  76.6 3.6 fusion.45
  80.3 2.6 gather_fusion
  83.0 3.5 fusion.45
  86.7 2.6 gather_fusion
  89.4 3.5 fusion.45
  93.1 2.6 gather_fusion
  95.8 3.6 fusion.45
  99.6 2.6 gather_fusion
  102.3 3.5 fusion.45
  106.0 2.6 gather_fusion
  108.6 0.1 copy.78
  108.7 3.5 fusion.45
  112.2 2.7 copy.51
  114.9 1.7 copy.70
  116.8 0.4 copy-done.8
  117.4 0.2 fusion.34
  117.6 219.8 %reduce-scatter.3.cloned.1.call-done = bf16[64,512]{1,0:T(8,128)(2,1)} async-done(((bf16[2048,512]{1,0:T(8,128)(2,1)}), bf16[64,512]{1,0:T(8,128)(2,1)}) %reduce-scatter.3.cloned.1.call-update) | async-done | bytes 65552 | tf_op jit(solution)/shard_map/reduce_scatter | solution.py:77
  337.5 1.5 fusion.32
  339.1 83.5 %all-gather.2.cloned.1.call-done = bf16[2048,512]{1,0:T(8,128)(2,1)} async-done(((bf16[64,512]{1,0:T(8,128)(2,1)}), bf16[2048,512]{1,0:T(8,128)(2,1)}) %all-gather.2.cloned.1.call-update) | async-done | bytes 2097168 | tf_op jit(solution)/shard_map/all_gather | solution.py:88
  422.6 4.0 reshape_reshape.9
  426.6 57.6 %while.21 = (s32[]{:T(128)}, bf16[8,8,32,384]{3,2,1,0:T(8,128)(2,1)}, bf16[8,8,32,4,128]{4,3,2,1,0:T(4,128)(2,1)}, s32[8,8,4]{1,2,0:T(4,128)S(1)}, bf16[12,128,384]{2,1,0:T(8,128)(2,1)S(1)}, /*index=5*/s32[]{:T(128)}) while((s32[]{:T(128)}, bf16[8,8,32,384]{3,2,1,0:T(8,128)(2,1)}, bf16[8,8,32,4,128]{4,3,2,1,0:T(4,128)(2,1)}, ...), condition=%wide.region_6.7_spmd, body=%wide.region_5.6_spmd.sunk | while | flops 102237472 | bytes 10622801 | solution.py:15
  426.7 2.6 gather_fusion.1
  429.5 1.0 constant_dynamic-slice_fusion.4
  430.5 3.3 fusion.47
  433.9 2.6 gather_fusion.1
  436.7 1.0 constant_dynamic-slice_fusion.4
  437.7 3.3 fusion.47
  441.2 2.6 gather_fusion.1
  443.9 1.0 constant_dynamic-slice_fusion.4
  444.9 3.3 fusion.47
  448.4 2.6 gather_fusion.1
  451.1 1.0 constant_dynamic-slice_fusion.4
  452.1 3.3 fusion.47
  455.6 2.6 gather_fusion.1
  458.3 1.0 constant_dynamic-slice_fusion.4
  459.3 3.2 fusion.47
  462.8 2.6 gather_fusion.1
  465.5 1.0 constant_dynamic-slice_fusion.4
  466.5 3.3 fusion.47
  470.0 2.6 gather_fusion.1
  472.7 1.0 constant_dynamic-slice_fusion.4
  473.7 3.2 fusion.47
  477.1 2.6 gather_fusion.1
  479.9 1.0 constant_dynamic-slice_fusion.4
  480.9 3.3 fusion.47
  484.2 42.5 %all_to_all.32 = bf16[32,64,384]{2,1,0:T(8,128)(2,1)S(1)} all-to-all(bf16[32,64,384]{2,1,0:T(8,128)(2,1)} %bitcast.117), channel_id=1, replica_groups=mesh['dp'=32,'tensor'=16] {'dp'}, dimensions={0} | all-to-all | bytes 3145728 | tf_op jit(solution)/shard_map/all_to_all | solution.py:91
  526.7 1.3 copy.60
  528.0 59.0 %reduce-scatter.5.cloned.1.call-done = bf16[64,768]{1,0:T(8,128)(2,1)} async-done(((bf16[64,12288]{1,0:T(8,128)(2,1)}), bf16[64,768]{1,0:T(8,128)(2,1)}) %reduce-scatter.5.cloned.1.call-update) | async-done | bytes 98320 | tf_op jit(solution)/shard_map/reduce_scatter | solution.py:92
  587.0 1.6 add_convert_fusion
  (132 shorter events, 5.1 us)
Async XLA Ops:
  6.5 110.9 %copy-start = (bf16[1536]{0:T(1024)(128)(2,1)S(1)}, bf16[1536]{0:T(1024)(128)(2,1)}, u32[]{:S(2)}) copy-start(bf16[1536]{0:T(1024)(128)(2,1)} %param.17) | copy-start | bytes 9220
  6.5 1.9 copy-start.2
  6.5 2.5 copy-start.4
  6.5 2.5 copy-start.5
  11.2 10.4 %copy-start.6 = (s32[64,1,4]{0,2,1:T(4,128)S(1)}, s32[64,1,4]{0,2,1:T(4,128)}, u32[]{:S(2)}) copy-start(s32[64,1,4]{0,2,1:T(4,128)} %param.20) | copy-start | bytes 3076
  11.2 10.5 %copy-start.3 = (bf16[384,1536]{1,0:T(8,128)(2,1)S(1)}, bf16[384,1536]{1,0:T(8,128)(2,1)}, u32[]{:S(2)}) copy-start(bf16[384,1536]{1,0:T(8,128)(2,1)} %param.16) | copy-start | bytes 3538948
  11.2 49.7 %all-to-all-start = ((bf16[64,32,384]{2,0,1:T(8,128)(2,1)}), bf16[64,32,384]{2,0,1:T(8,128)(2,1)}, u32[]{:S(2)}, u32[]{:S(2)}) async-start(bf16[64,32,384]{2,0,1:T(8,128)(2,1)} %bitcast.85), calls=%async_computation | async-start | bytes 3145728 | tf_op jit(solution)/shard_map/all_to_all | solution.py:69
  21.6 315.8 %reduce-scatter.3.cloned.1.call-start = ((), (), s32[]{:S(2)}) async-start(), calls=%async_computation.4 | async-start | bytes 2162688 | tf_op jit(solution)/shard_map/reduce_scatter | solution.py:77
  116.6 0.7 copy-start.8
  116.6 306.0 %all-gather.2.cloned.1.call-start = ((), (), s32[]{:S(2)}) async-start(), calls=%async_computation.5 | async-start | bytes 2162688 | tf_op jit(solution)/shard_map/all_gather | solution.py:88
  339.0 248.0 %reduce-scatter.5.cloned.1.call-start = ((), (), s32[]{:S(2)}) async-start(), calls=%async_computation.6 | async-start | bytes 1671168 | tf_op jit(solution)/shard_map/reduce_scatter | solution.py:92
  339.1 87.5 %copy-start.1 = (bf16[1536,384]{1,0:T(8,128)(2,1)S(1)}, bf16[1536,384]{1,0:T(8,128)(2,1)}, u32[]{:S(2)}) copy-start(bf16[1536,384]{1,0:T(8,128)(2,1)} %param.18) | copy-start | bytes 3538948
  526.7 1.4 copy-start.7
Sparse Core Ops, SparseCore 0:
  116.7 220.6 reduce-scatter.2
  341.0 81.5 all-gather.1
  528.1 58.8 reduce-scatter.4
where the time goes:
time: 596 us; the launch traced here: 595 us
  waiting for transfers between devices  398 us (67%)
  local copies, waits for them, and re-layouts  69.3 us (12%)
  matrix products  54.5 us (9%)
  blocking collectives  42.5 us (7%)
  between operations  13.3 us (2%)
  starting transfers between devices  10.5 us (2%)
  other arithmetic  6.56 us (1%)
    reduce_scatter x1, waiting for transfers between devices, body(): lax.psum_scatter(select_up(columns, ids, up_table).astype(jnp.bfloat16),...  220 us
    all_gather x1, waiting for transfers between devices, body(): act = lax.all_gather(act_own, 'dp', axis=0, tiled=True)  83.5 us
    reduce_scatter x1, waiting for transfers between devices, body(): lax.psum_scatter(returned.astype(jnp.float32).astype(jnp.bfloat16), 'tens...  59 us
    all_to_all x1, blocking collectives, body(): lax.all_to_all(branch, 'dp', split_axis=0, concat_axis=1, tiled=True)  42.5 us
    all_to_all x1, waiting for transfers between devices, body(): lax.all_to_all(normed, 'dp', split_axis=1, concat_axis=0, tiled=True)  36.1 us
    dot_general x8, matrix products, step(): jnp.einsum('grd,dgcb->grcb', block_rows, chosen, preferred_element_type=j...  28.3 us
    dot_general x8, matrix products, step(): jnp.einsum('grcb,gcbd->grd', block_act, chosen, preferred_element_type=jn...  26 us
    gather x8, local copies, waits for them, and re-layouts, step(): chosen = jnp.take(down_table, block_ids, axis=0)  20.9 us
  transfers between devices with their start and end apart: 4, of which 4 were waited for; matrix products, arithmetic and copies ran while one was open for 1% of the time, Pallas kernels for 0%

commit v1 on v0

--- a/solution.py
+++ b/solution.py
@@ -85,7 +85,9 @@
     own_ids = lax.dynamic_slice_in_dim(ids, first, per_dev, 0)
     own_valid = lax.dynamic_slice_in_dim(valid, first, per_dev, 0)
     act_own = activate(pre_own, own_ids, own_valid, bias_table)
-    act = lax.all_gather(act_own, "dp", axis=0, tiled=True)
+    act = lax.all_to_all(
+        jnp.concatenate(lax.axis_size("dp") * [act_own], axis=0), "dp", 0, 0, tiled=True
+    )
     branch = select_down(act, ids, down_table)
     branch = branch.astype(jnp.bfloat16)
     returned = lax.all_to_all(branch, "dp", split_axis=0, concat_axis=1, tiled=True)

time: 596 us -> 566 us (0.950)
  waiting for transfers between devices: 398 us -> 359 us
  starting transfers between devices: 10.5 us -> 18.7 us
    all_gather x1 -> x0, waiting for transfers between devices: 83.5 us -> none  [body(): act = lax.all_gather(act_own, 'dp', axis=0, tiled=True)]
    all_to_all x0 -> x1, waiting for transfers between devices: none -> 44.6 us  [body(): lax.all_to_all(jnp.concatenate(lax.axis_size('dp') * [act_own], axis=0),...]
    all_to_all x0 -> x1, starting transfers between devices: none -> 8.25 us  [body(): lax.all_to_all(jnp.concatenate(lax.axis_size('dp') * [act_own], axis=0),...]
where the time goes in v1:
time: 566 us; the launch traced here: 565 us
  waiting for transfers between devices  359 us (63%)
  local copies, waits for them, and re-layouts  70.8 us (13%)
  matrix products  54.5 us (10%)
  blocking collectives  41.9 us (7%)
  starting transfers between devices  18.7 us (3%)
  between operations  13.8 us (2%)
  other arithmetic  5.93 us (1%)
    reduce_scatter x1, waiting for transfers between devices, body(): lax.psum_scatter(select_up(columns, ids, up_table).astype(jnp.bfloat16),...  220 us
    reduce_scatter x1, waiting for transfers between devices, body(): lax.psum_scatter(returned.astype(jnp.float32).astype(jnp.bfloat16), 'tens...  58.9 us
    all_to_all x1, waiting for transfers between devices, body(): lax.all_to_all(jnp.concatenate(lax.axis_size('dp') * [act_own], axis=0),...  44.6 us
    all_to_all x1, blocking collectives, body(): lax.all_to_all(branch, 'dp', split_axis=0, concat_axis=1, tiled=True)  41.9 us
    all_to_all x1, waiting for transfers between devices, body(): lax.all_to_all(normed, 'dp', split_axis=1, concat_axis=0, tiled=True)  36.1 us
    dot_general x8, matrix products, step(): jnp.einsum('grd,dgcb->grcb', block_rows, chosen, preferred_element_type=j...  28.3 us
    dot_general x8, matrix products, step(): jnp.einsum('grcb,gcbd->grd', block_act, chosen, preferred_element_type=jn...  26 us
    gather x8, local copies, waits for them, and re-layouts, step(): chosen = jnp.take(down_table, block_ids, axis=0)  20.9 us
  transfers between devices with their start and end apart: 4, of which 4 were waited for; matrix products, arithmetic and copies ran while one was open for 1% of the time, Pallas kernels for 0%

profile of v1, /device:TPU:6, one launch (start us, length us, event | category | flops | bytes accessed | tf_op | source)
XLA Modules:
  0.0 565.2 jit_solution(15619108084589416661)
XLA Ops:
  6.5 1.8 convert_reduce_fusion
  8.4 0.6 fusion.28
  9.1 0.6 fusion.31
  9.8 1.4 copy.73
  11.2 10.4 %all-to-all-start = ((bf16[64,32,384]{2,0,1:T(8,128)(2,1)}), bf16[64,32,384]{2,0,1:T(8,128)(2,1)}, u32[]{:S(2)}, u32[]{:S(2)}) async-start(bf16[64,32,384]{2,0,1:T(8,128)(2,1)} %bitcast.88), calls=%async_computation | async-start | bytes 3145728 | tf_op jit(solution)/shard_map/all_to_all | solution.py:69
  21.7 1.4 copy.48
  23.1 1.7 copy.50
  24.8 36.1 %all-to-all-done = bf16[64,32,384]{2,0,1:T(8,128)(2,1)} async-done(((bf16[64,32,384]{2,0,1:T(8,128)(2,1)}), bf16[64,32,384]{2,0,1:T(8,128)(2,1)}, u32[]{:S(2)}, u32[]{:S(2)}) %all-to-all-start) | async-done | bytes 1572896 | tf_op jit(solution)/shard_map/all_to_all | solution.py:69
  60.9 51.3 %while.20 = (s32[]{:T(128)}, bf16[8,8,32,4,128]{4,2,3,1,0:T(8,128)(2,1)}, bf16[8,8,32,384]{3,2,1,0:T(8,128)(2,1)}, s32[8,8,4]{1,2,0:T(4,128)S(1)}, bf16[384,12,128]{2,0,1:T(8,128)(2,1)S(1)}, /*index=5*/s32[]{:T(128)}) while((s32[]{:T(128)}, bf16[8,8,32,4,128]{4,2,3,1,0:T(8,128)(2,1)}, bf16[8,8,32,384]{3,2,1,0:T(8,128)(2,1)}, ...), condition=%wide.region_3.4_spmd, body=%wide.region_2.3_spmd.sunk | while | flops 102237472 | bytes 10164557 | solution.py:15
  61.1 2.6 gather_fusion
  63.8 3.5 fusion.46
  67.5 2.6 gather_fusion
  70.2 3.6 fusion.46
  73.9 2.6 gather_fusion
  76.6 3.5 fusion.46
  80.4 2.6 gather_fusion
  83.0 3.5 fusion.46
  86.7 2.6 gather_fusion
  89.4 3.5 fusion.46
  93.2 2.6 gather_fusion
  95.8 3.5 fusion.46
  99.6 2.6 gather_fusion
  102.2 3.5 fusion.46
  106.0 2.6 gather_fusion
  108.7 3.5 fusion.46
  112.2 2.7 copy.51
  114.9 1.7 copy.72
  116.8 0.5 copy-done.9
  117.4 0.2 fusion.34
  117.6 219.8 %reduce-scatter.3.cloned.1.call-done = bf16[64,512]{1,0:T(8,128)(2,1)} async-done(((bf16[2048,512]{1,0:T(8,128)(2,1)}), bf16[64,512]{1,0:T(8,128)(2,1)}) %reduce-scatter.3.cloned.1.call-update) | async-done | bytes 65552 | tf_op jit(solution)/shard_map/reduce_scatter | solution.py:77
  337.5 0.9 constant_dynamic-update-slice_fusion.31
  338.8 1.3 copy-done.3
  340.1 8.2 %all-to-all-start.1 = ((bf16[32,64,512]{2,1,0:T(8,128)(2,1)}), bf16[32,64,512]{2,1,0:T(8,128)(2,1)}, u32[]{:S(2)}, u32[]{:S(2)}) async-start(bf16[32,64,512]{2,1,0:T(8,128)(2,1)} %bitcast.120), calls=%async_computation.2 | async-start | bytes 4194304 | tf_op jit(solution)/shard_map/all_to_all | solution.py:88
  348.5 44.6 %all-to-all-done.1 = bf16[32,64,512]{2,1,0:T(8,128)(2,1)} async-done(((bf16[32,64,512]{2,1,0:T(8,128)(2,1)}), bf16[32,64,512]{2,1,0:T(8,128)(2,1)}, u32[]{:S(2)}, u32[]{:S(2)}) %all-to-all-start.1) | async-done | bytes 2097184 | tf_op jit(solution)/shard_map/all_to_all | solution.py:88
  393.1 4.0 reshape_reshape.9
  397.1 57.5 %while.21 = (s32[]{:T(128)}, bf16[8,8,32,384]{3,2,1,0:T(8,128)(2,1)}, bf16[8,8,32,4,128]{4,3,2,1,0:T(4,128)(2,1)}, s32[8,8,4]{1,2,0:T(4,128)S(1)}, bf16[12,128,384]{2,1,0:T(8,128)(2,1)S(1)}, /*index=5*/s32[]{:T(128)}) while((s32[]{:T(128)}, bf16[8,8,32,384]{3,2,1,0:T(8,128)(2,1)}, bf16[8,8,32,4,128]{4,3,2,1,0:T(4,128)(2,1)}, ...), condition=%wide.region_6.7_spmd, body=%wide.region_5.6_spmd.sunk | while | flops 102237472 | bytes 10622801 | solution.py:15
  397.2 2.6 gather_fusion.1
  400.0 1.0 constant_dynamic-slice_fusion.4
  401.0 3.3 fusion.48
  404.4 2.6 gather_fusion.1
  407.2 1.0 constant_dynamic-slice_fusion.4
  408.2 3.3 fusion.48
  411.6 2.6 gather_fusion.1
  414.4 1.0 constant_dynamic-slice_fusion.4
  415.4 3.3 fusion.48
  418.8 2.6 gather_fusion.1
  421.6 1.0 constant_dynamic-slice_fusion.4
  422.6 3.3 fusion.48
  426.0 2.6 gather_fusion.1
  428.8 1.0 constant_dynamic-slice_fusion.4
  429.8 3.2 fusion.48
  433.2 2.6 gather_fusion.1
  435.9 1.0 constant_dynamic-slice_fusion.4
  437.0 3.2 fusion.48
  440.4 2.6 gather_fusion.1
  443.1 1.0 constant_dynamic-slice_fusion.4
  444.2 3.2 fusion.48
  447.6 2.6 gather_fusion.1
  450.3 1.0 constant_dynamic-slice_fusion.4
  451.4 3.2 fusion.48
  454.6 41.9 %all_to_all.41 = bf16[32,64,384]{2,1,0:T(8,128)(2,1)S(1)} all-to-all(bf16[32,64,384]{2,1,0:T(8,128)(2,1)} %bitcast.121), channel_id=1, replica_groups=mesh['dp'=32,'tensor'=16] {'dp'}, dimensions={0} | all-to-all | bytes 3145728 | tf_op jit(solution)/shard_map/all_to_all | solution.py:93
  496.5 1.3 copy.60
  497.9 58.9 %reduce-scatter.5.cloned.1.call-done = bf16[64,768]{1,0:T(8,128)(2,1)} async-done(((bf16[64,12288]{1,0:T(8,128)(2,1)}), bf16[64,768]{1,0:T(8,128)(2,1)}) %reduce-scatter.5.cloned.1.call-update) | async-done | bytes 98320 | tf_op jit(solution)/shard_map/reduce_scatter | solution.py:94
  556.8 1.6 add_convert_fusion
  (164 shorter events, 5.5 us)
Async XLA Ops:
  6.5 110.8 %copy-start = (bf16[1536]{0:T(1024)(128)(2,1)S(1)}, bf16[1536]{0:T(1024)(128)(2,1)}, u32[]{:S(2)}) copy-start(bf16[1536]{0:T(1024)(128)(2,1)} %param.17) | copy-start | bytes 9220
  6.5 1.9 copy-start.2
  6.5 2.5 copy-start.5
  6.5 2.5 copy-start.6
  11.2 10.4 %copy-start.7 = (s32[64,1,4]{0,2,1:T(4,128)S(1)}, s32[64,1,4]{0,2,1:T(4,128)}, u32[]{:S(2)}) copy-start(s32[64,1,4]{0,2,1:T(4,128)} %param.20) | copy-start | bytes 3076
  11.2 10.5 %copy-start.4 = (bf16[384,1536]{1,0:T(8,128)(2,1)S(1)}, bf16[384,1536]{1,0:T(8,128)(2,1)}, u32[]{:S(2)}) copy-start(bf16[384,1536]{1,0:T(8,128)(2,1)} %param.16) | copy-start | bytes 3538948
  11.2 49.7 %all-to-all-start = ((bf16[64,32,384]{2,0,1:T(8,128)(2,1)}), bf16[64,32,384]{2,0,1:T(8,128)(2,1)}, u32[]{:S(2)}, u32[]{:S(2)}) async-start(bf16[64,32,384]{2,0,1:T(8,128)(2,1)} %bitcast.88), calls=%async_computation | async-start | bytes 3145728 | tf_op jit(solution)/shard_map/all_to_all | solution.py:69
  21.6 315.8 %reduce-scatter.3.cloned.1.call-start = ((), (), s32[]{:S(2)}) async-start(), calls=%async_computation.5 | async-start | bytes 2162688 | tf_op jit(solution)/shard_map/reduce_scatter | solution.py:77
  116.6 0.7 copy-start.9
  338.8 1.3 copy-start.3
  340.1 52.9 %all-to-all-start.1 = ((bf16[32,64,512]{2,1,0:T(8,128)(2,1)}), bf16[32,64,512]{2,1,0:T(8,128)(2,1)}, u32[]{:S(2)}, u32[]{:S(2)}) async-start(bf16[32,64,512]{2,1,0:T(8,128)(2,1)} %bitcast.120), calls=%async_computation.2 | async-start | bytes 4194304 | tf_op jit(solution)/shard_map/all_to_all | solution.py:88
  348.4 208.4 %reduce-scatter.5.cloned.1.call-start = ((), (), s32[]{:S(2)}) async-start(), calls=%async_computation.6 | async-start | bytes 1671168 | tf_op jit(solution)/shard_map/reduce_scatter | solution.py:94
  348.5 48.6 %copy-start.1 = (bf16[1536,384]{1,0:T(8,128)(2,1)S(1)}, bf16[1536,384]{1,0:T(8,128)(2,1)}, u32[]{:S(2)}) copy-start(bf16[1536,384]{1,0:T(8,128)(2,1)} %param.18) | copy-start | bytes 3538948
  496.5 1.4 copy-start.8
Sparse Core Ops, SparseCore 0:
  116.7 220.6 reduce-scatter.2
  498.0 58.7 reduce-scatter.4
